TPU v7x, 32 devices: a whole 2x2x4 slice. The times are simulated.
32 devices in a mesh: groups: 2 (over x), aux: 16 (over z, y, core).
Axes of the slice: x: 2, y: 2, z: 4, core: 2. Of those that a mesh axis runs over, the one named last changes fastest.
Arguments:
- integrals: bfloat16 [1024, 3, 128, 3, 128], P(('groups', 'aux')), parts along dimension 0, may hold values from -0.3125 to 0.3125
- coeff: bfloat16 [8192, 1024], P(('groups', 'aux')), parts along dimension 0, may hold values from -0.046875 to 0.046875
- screen: int32 [32, 3], P(('groups', 'aux')), parts along dimension 0, may hold values from 0 to 5, as said below
- occ_ids: int32 [8], P('groups'), parts along dimension 0, may hold values from 0 to 7, as said below
Outputs:
- exchange_band: float32 [8192, 1280], P(('groups', 'aux')), parts along dimension 0
There are 2 independent parts, one for each index of `groups`. A program takes and returns all parts, laid end to end along the dimension named above; each array names one. Nothing has to cross between parts.
Inputs may be any that keep to these rules, and one draw needn't show every extreme that they name: `screen`: each row holds 3 distinct positions, and 2 * row - 2 + value is always a basis block of the molecule. `occ_ids`: distinct occupied block ids.
All inputs are finite; a program needn't handle non-finite values.
Results may differ from a plain program's by a relative error of at most 0.00054.
Values may be sent and summed in bfloat16 or wider, within the bound.
A program may use at most 128 MiB of HBM per device.

v0:
```python
import jax
import jax.numpy as jnp
from jax import lax
from jax.sharding import PartitionSpec as P

BLK = 128
BB_DEV = 2
NSB = 3
OCCB = 4
OCCA_B = 8


def with_halo(cells, sides, width):
    for axis, dim in sides:
        count = lax.axis_size(axis)
        ends = count - 1
        head = lax.slice_in_dim(cells, 0, width, axis=dim)
        tail = lax.slice_in_dim(cells, cells.shape[dim] - width, cells.shape[dim], axis=dim)
        cells = jnp.concatenate(
            [
                lax.ppermute(tail, axis, [(i, (i + 1) % count) for i in range(ends)]),
                cells,
                lax.ppermute(head, axis, [((i + 1) % count, i) for i in range(ends)]),
            ],
            axis=dim,
        )
    return cells


def passed_along(block, axis, distance):
    devices = range(lax.axis_size(axis))
    route = [(i - distance, i) for i in devices if i - distance in devices]
    return lax.ppermute(block, axis, route)


def shards(integrals, coeff, screen, occ_ids):
    rows_own = coeff.shape[0]
    edge = BB_DEV * BLK
    occupied = jnp.take(coeff.reshape(rows_own, OCCA_B, BLK), occ_ids, axis=1).reshape(
        rows_own, OCCB * BLK
    )
    window_ids = screen[0]
    window = with_halo(occupied, (("aux", 0),), edge)
    picked = jnp.take(window.reshape(3 * BB_DEV, BLK, OCCB * BLK), window_ids, axis=0)
    aux_rows = integrals.shape[0]
    half = jnp.dot(
        integrals.reshape(aux_rows * NSB * BLK, NSB * BLK),
        picked.reshape(NSB * BLK, OCCB * BLK),
        preferred_element_type=jnp.float32,
    )
    half = half.astype(jnp.bfloat16).reshape(aux_rows, NSB * BLK, OCCB * BLK)
    partial_value = lax.dot_general(
        half, half, (((0, 2), (0, 2)), ((), ())), preferred_element_type=jnp.float32
    )
    partial_value = partial_value.reshape(NSB, BLK, NSB, BLK)
    placed = jnp.zeros((3 * edge, 3 * edge), jnp.float32)
    for first in range(NSB):
        start_row = window_ids[first] * BLK
        for second in range(NSB):
            start_col = window_ids[second] * BLK
            placed = lax.dynamic_update_slice(
                placed, partial_value[first, :, second, :], (start_row, start_col)
            )
    from_prev = passed_along(placed[2 * edge :], "aux", 1)
    from_next = passed_along(placed[:edge], "aux", -1)
    band = jnp.zeros((edge, 5 * edge), jnp.float32)
    band = band.at[:, 0 : 3 * edge].add(from_prev)
    band = band.at[:, edge : 4 * edge].add(placed[edge : 2 * edge])
    band = band.at[:, 2 * edge : 5 * edge].add(from_next)
    return band


def solution(mesh):
    return jax.shard_map(
        shards,
        mesh=mesh,
        in_specs=(
            P(("groups", "aux"), None, None, None, None),
            P(("groups", "aux"), None),
            P(("groups", "aux"), None),
            P("groups"),
        ),
        out_specs=P(("groups", "aux"), None),
        check_vma=False,
    )
```

profile of v0, /device:TPU:1, one launch (start us, length us, event | category | flops | bytes accessed | tf_op | source)
XLA Modules:
  0.0 165.1 jit_solution(16663945746272533302)
XLA Ops:
  0.0 0.0 copy-start.1
  0.0 0.7 compare_select_fusion.1
  0.7 0.7 compare_and_fusion
  1.3 1.2 copy.16
  2.6 0.3 copy.17
  2.9 0.6 gather_fusion
  3.5 0.1 copy.18
  3.6 0.1 broadcast_bitcast_fusion
  3.7 0.1 bitcast_select_fusion
  3.8 4.5 %collective-permute-start = (bf16[256,512]{0,1:T(8,128)(2,1)S(1)}, bf16[256,512]{0,1:T(8,128)(2,1)S(1)}, u32[]{:S(2)}, u32[]{:S(2)}) collective-permute-start(bf16[256,512]{0,1:T(8,128)(2,1)S(1)} %bitcast_select_fusion), channel_id=1, source_target_pairs={{0,1},{1,2},{2,3},{3,4},{4,5},{5,6},{6,7},{7,8},{8,9},{9,10},{10,1... | collective-permute-start | bytes 786440 | tf_op jit(solution)/shard_map/ppermute | solution.py:21
  8.4 1.9 %collective-permute-start.1 = (bf16[256,512]{0,1:T(8,128)(2,1)S(1)}, bf16[256,512]{0,1:T(8,128)(2,1)S(1)}, u32[]{:S(2)}, u32[]{:S(2)}) collective-permute-start(bf16[256,512]{0,1:T(8,128)(2,1)S(1)} %bitcast_select_fusion), channel_id=1, source_target_pairs={{1,0},{2,1},{3,2},{4,3},{5,4},{6,5},{7,6},{8,7},{9,8},{10,9},{11,1... | collective-permute-start | bytes 786440 | tf_op jit(solution)/shard_map/ppermute | solution.py:23
  10.3 0.0 copy-done.1
  10.3 0.7 fusion.24
  12.9 13.9 %copy.20 = bf16[32,3,128,3,128]{4,3,2,1,0:T(4,128)(2,1)} copy(bf16[32,3,128,3,128]{4,2,3,1,0:T(8,128)(2,1)} %param.10) | data formatting | bytes 18874368 | tf_op args[0]
  26.8 0.0 collective-permute-done
  26.8 0.0 collective-permute-done.1
  26.8 0.1 pad_maximum_fusion
  26.9 0.3 copy.19
  27.2 0.6 gather_fusion.1
  27.8 0.1 broadcast_select_fusion.1
  27.9 14.2 %convolution_convert_fusion = bf16[512,12288]{1,0:T(8,128)(2,1)} fusion(bf16[384,512]{1,0:T(8,128)(2,1)S(1)} %bitcast.85, bf16[1536,8,3,128]{3,2,1,0:T(4,128)(2,1)} %bitcast.81), kind=kOutput, calls=%fused_computation.2 | convolution fusion | flops 4838129664 | bytes 22413312 | tf_op jit(solution)/shard_map/dot_general | solution.py:46
  42.1 11.5 %copy.29 = bf16[64,8,32,384]{3,2,1,0:T(8,128)(2,1)} copy(bf16[64,8,32,384]{3,1,2,0:T(8,128)(2,1)} %bitcast.78) | data formatting | bytes 25165824
  53.6 18.0 %copy.21 = bf16[32,384,512]{2,0,1:T(8,128)(2,1)} copy(bf16[32,384,512]{1,0,2:T(8,128)(2,1)} %bitcast.77) | data formatting | bytes 25165824 | tf_op jit(solution)/shard_map/reshape | solution.py:51
  71.6 62.5 %fusion.6 = f32[3,128,3,128]{3,1,2,0:T(8,128)S(1)} fusion(bf16[3,128,32,512]{3,2,1,0:T(8,128)(2,1)} %bitcast.79, bf16[3,128,32,512,1]{3,2,1,0,4:T(8,128)(2,1)} %bitcast.80), kind=kOutput, calls=%fused_computation.9 | convolution fusion | flops 4831838208 | bytes 25755648 | tf_op jit(solution)/shard_map/dot_general | solution.py:52
  134.1 0.2 broadcast_in_dim.30
  134.5 0.1 slice.141
  134.6 3.6 %collective-permute-start.2 = (f32[256,768]{1,0:T(8,128)S(1)}, f32[256,768]{1,0:T(8,128)S(1)}, u32[]{:S(2)}, u32[]{:S(2)}) collective-permute-start(f32[256,768]{1,0:T(8,128)S(1)} %slice.141), channel_id=1, source_target_pairs={{0,1},{1,2},{2,3},{3,4},{4,5},{5,6},{6,7},{7,8},{8,9},{9,10},{10,1... | collective-permute-start | bytes 2359304 | tf_op jit(solution)/shard_map/ppermute | solution.py:33
  138.2 0.6 compare_reduce_fusion.1
  138.8 0.7 compare_reduce_fusion
  139.5 7.6 %collective-permute-done.2 = f32[256,768]{1,0:T(8,128)S(1)} collective-permute-done((f32[256,768]{1,0:T(8,128)S(1)}, f32[256,768]{1,0:T(8,128)S(1)}, u32[]{:S(2)}, u32[]{:S(2)}) %collective-permute-start.2) | collective-permute-done | bytes 786464 | tf_op jit(solution)/shard_map/ppermute | solution.py:33
  147.1 0.7 broadcast_select_fusion
  147.8 0.1 scatter-add.10
  147.9 1.0 fusion.23
  149.0 0.0 copy-start
  149.0 1.9 %collective-permute-start.3 = (f32[256,768]{1,0:T(8,128)S(1)}, f32[256,768]{1,0:T(8,128)S(1)}, u32[]{:S(2)}, u32[]{:S(2)}) collective-permute-start(f32[256,768]{1,0:T(8,128)S(1)} %get-tuple-element.41), channel_id=1, source_target_pairs={{1,0},{2,1},{3,2},{4,3},{5,4},{6,5},{7,6},{8,7},{9,8},{10,9},{11,1... | collective-permute-start | bytes 2359304 | tf_op jit(solution)/shard_map/ppermute | solution.py:33
  150.9 12.1 %collective-permute-done.3 = f32[256,768]{1,0:T(8,128)S(1)} collective-permute-done((f32[256,768]{1,0:T(8,128)S(1)}, f32[256,768]{1,0:T(8,128)S(1)}, u32[]{:S(2)}, u32[]{:S(2)}) %collective-permute-start.3) | collective-permute-done | bytes 786464 | tf_op jit(solution)/shard_map/ppermute | solution.py:33
  163.0 0.0 copy-done
  163.0 2.1 %fusion.12 = f32[256,1280]{1,0:T(8,128)} fusion(f32[256,1280]{1,0:T(8,128)} %copy-done, f32[256,768]{1,0:T(8,128)S(1)} %collective-permute-done.3), kind=kLoop, calls=%fused_computation.13 | loop fusion | flops 196608 | bytes 2359296 | tf_op jit(solution)/shard_map/scatter-add | solution.py:69
  (13 shorter events, 0.1 us)
Async XLA Ops:
  0.0 10.3 %copy-start.1 = (s32[1,3]{1,0:T(1,128)S(1)}, s32[1,3]{1,0:T(1,128)}, u32[]{:S(2)}) copy-start(s32[1,3]{1,0:T(1,128)} %param.12) | copy-start | bytes 40
  3.8 23.0 %collective-permute-start = (bf16[256,512]{0,1:T(8,128)(2,1)S(1)}, bf16[256,512]{0,1:T(8,128)(2,1)S(1)}, u32[]{:S(2)}, u32[]{:S(2)}) collective-permute-start(bf16[256,512]{0,1:T(8,128)(2,1)S(1)} %bitcast_select_fusion), channel_id=1, source_target_pairs={{0,1},{1,2},{2,3},{3,4},{4,5},{5,6},{6,7},{7,8},{8,9},{9,10},{10,1... | collective-permute-start | bytes 786440 | tf_op jit(solution)/shard_map/ppermute | solution.py:21
  8.4 18.4 %collective-permute-start.1 = (bf16[256,512]{0,1:T(8,128)(2,1)S(1)}, bf16[256,512]{0,1:T(8,128)(2,1)S(1)}, u32[]{:S(2)}, u32[]{:S(2)}) collective-permute-start(bf16[256,512]{0,1:T(8,128)(2,1)S(1)} %bitcast_select_fusion), channel_id=1, source_target_pairs={{1,0},{2,1},{3,2},{4,3},{5,4},{6,5},{7,6},{8,7},{9,8},{10,9},{11,1... | collective-permute-start | bytes 786440 | tf_op jit(solution)/shard_map/ppermute | solution.py:23
  134.6 12.6 %collective-permute-start.2 = (f32[256,768]{1,0:T(8,128)S(1)}, f32[256,768]{1,0:T(8,128)S(1)}, u32[]{:S(2)}, u32[]{:S(2)}) collective-permute-start(f32[256,768]{1,0:T(8,128)S(1)} %slice.141), channel_id=1, source_target_pairs={{0,1},{1,2},{2,3},{3,4},{4,5},{5,6},{6,7},{7,8},{8,9},{9,10},{10,1... | collective-permute-start | bytes 2359304 | tf_op jit(solution)/shard_map/ppermute | solution.py:33
  149.0 14.1 %copy-start = (f32[256,1280]{1,0:T(8,128)}, f32[256,1280]{1,0:T(8,128)S(1)}, u32[]{:S(2)}) copy-start(f32[256,1280]{1,0:T(8,128)S(1)} %get-tuple-element.42) | copy-start | bytes 3932164
  149.0 14.1 %collective-permute-start.3 = (f32[256,768]{1,0:T(8,128)S(1)}, f32[256,768]{1,0:T(8,128)S(1)}, u32[]{:S(2)}, u32[]{:S(2)}) collective-permute-start(f32[256,768]{1,0:T(8,128)S(1)} %get-tuple-element.41), channel_id=1, source_target_pairs={{1,0},{2,1},{3,2},{4,3},{5,4},{6,5},{7,6},{8,7},{9,8},{10,9},{11,1... | collective-permute-start | bytes 2359304 | tf_op jit(solution)/shard_map/ppermute | solution.py:33
where the time goes:
time: 167 us; the launch traced here: 165 us
  matrix products  76.7 us (46%)
  local copies, waits for them, and re-layouts  47.7 us (29%)
  waiting for transfers between devices  19.7 us (12%)
  starting transfers between devices  12 us (7%)
  other arithmetic  6.82 us (4%)
  between operations  2.16 us (1%)
    dot_general x1, matrix products, shards(): lax.dot_general(half, half, (((0, 2), (0, 2)), ((), ())), preferred_eleme...  62.5 us
    unnamed x7, local copies, waits for them, and re-layouts  26.7 us
    ppermute x2, waiting for transfers between devices, passed_along(): return lax.ppermute(block, axis, route)  19.7 us
    reshape x1, local copies, waits for them, and re-layouts, shards(): half = half.astype(jnp.bfloat16).reshape(aux_rows, NSB * BLK, OCCB * BLK)  18 us
    dot_general x1, matrix products, shards(): jnp.dot(integrals.reshape(aux_rows * NSB * BLK, NSB * BLK), picked.reshap...  14.2 us
    ppermute x2, starting transfers between devices, passed_along(): return lax.ppermute(block, axis, route)  5.56 us
    ppermute x1, starting transfers between devices, with_halo(): lax.ppermute(tail, axis, [(i, (i + 1) % count) for i in range(ends)])  4.54 us
  transfers between devices with their start and end apart: 4, of which 2 were waited for; matrix products, arithmetic and copies ran while one was open for 10% of the time, Pallas kernels for 0%

commit v1 on v0

v1 whole, which is shorter than its diff:
```python
import jax
import jax.numpy as jnp
from jax import lax
from jax.experimental import pallas as pl
from jax.experimental.pallas import tpu as pltpu
from jax.sharding import PartitionSpec as P

BLK = 128
BB_DEV = 2
NSB = 3
OCCB = 4
OCCA_B = 8
EDGE = BB_DEV * BLK
STEP = 2
MIB = 1 << 20


def kernel(count, ints, coeff, screen, occ_ids, band, buf, window, picked, total, ext, out_prev, out_next,
           in_prev, in_next, ids_prev, ids_next, load_sem, occ_send, occ_recv, id_send, id_recv, row_send, row_recv):
    me = lax.axis_index("aux")
    has_prev, has_next = me > 0, me < count - 1
    aux_rows = ints.shape[0]
    steps = aux_rows // STEP

    barrier = pltpu.get_barrier_semaphore()

    @pl.when(has_prev)
    def _():
        pl.semaphore_signal(barrier, inc=1, device_id={"aux": me - 1}, device_id_type=pl.DeviceIdType.MESH)

    @pl.when(has_next)
    def _():
        pl.semaphore_signal(barrier, inc=1, device_id={"aux": me + 1}, device_id_type=pl.DeviceIdType.MESH)

    def load(step):
        part = pl.ds(step * STEP, STEP)
        return pltpu.make_async_copy(ints.at[part], buf.at[part], load_sem.at[step])

    @pl.loop(0, steps)
    def _(step):
        load(step).start()

    def pick(index, blocks):
        return sum(block * (index == k).astype(jnp.float32).astype(block.dtype) for k, block in enumerate(blocks))

    for o in range(OCCB):
        chosen = pick(occ_ids[o], [coeff[:, k * BLK : (k + 1) * BLK] for k in range(OCCA_B)])
        for r in range(BB_DEV):
            window[BB_DEV + r, :, o * BLK : (o + 1) * BLK] = chosen[r * BLK : (r + 1) * BLK]

    def remote(src, dst, send, recv, device):
        return pltpu.make_async_remote_copy(
            src_ref=src, dst_ref=dst, send_sem=send, recv_sem=recv,
            device_id={"aux": device}, device_id_type=pl.DeviceIdType.MESH)

    own = window.at[BB_DEV : 2 * BB_DEV]
    occ_down = remote(own, window.at[2 * BB_DEV : 3 * BB_DEV], occ_send.at[0], occ_recv.at[0], me - 1)
    occ_up = remote(own, window.at[0:BB_DEV], occ_send.at[1], occ_recv.at[1], me + 1)
    id_down = remote(screen, ids_next, id_send.at[0], id_recv.at[0], me - 1)
    id_up = remote(screen, ids_prev, id_send.at[1], id_recv.at[1], me + 1)

    pl.semaphore_wait(barrier, has_prev.astype(jnp.int32) + has_next.astype(jnp.int32))

    @pl.when(has_prev)
    def _():
        occ_down.start()
        id_down.start()

    @pl.when(has_next)
    def _():
        occ_up.start()
        id_up.start()

    total[...] = jnp.zeros_like(total)
    zero = jnp.zeros((BLK, BLK), jnp.float32)
    @pl.when(has_next)
    def _():
        occ_down.wait_recv()

    @pl.when(jnp.logical_not(has_next))
    def _():
        window[2 * BB_DEV : 3 * BB_DEV] = jnp.zeros((BB_DEV, BLK, OCCB * BLK), window.dtype)

    @pl.when(has_prev)
    def _():
        occ_up.wait_recv()

    @pl.when(jnp.logical_not(has_prev))
    def _():
        window[0:BB_DEV] = jnp.zeros((BB_DEV, BLK, OCCB * BLK), window.dtype)

    for t in range(NSB):
        picked[t * BLK : (t + 1) * BLK] = pick(screen[0, t], [window[w] for w in range(3 * BB_DEV)])

    nt = (((1,), (1,)), ((), ()))

    @pl.loop(0, steps)
    def _(step):
        load(step).wait()
        halves = []
        for p in range(STEP):
            x = buf[step * STEP + p]
            left = jnp.concatenate([x[:, t].reshape(NSB * BLK, BLK) for t in range(NSB)], axis=1)
            halves.append(jnp.dot(left, picked[...], preferred_element_type=jnp.float32).astype(jnp.bfloat16))
        half = jnp.concatenate(halves, axis=1)
        low = half[: 2 * BLK]
        high = half[2 * BLK :]
        total[:, : 2 * BLK] += lax.dot_general(half, low, nt, preferred_element_type=jnp.float32)
        total[2 * BLK :, 2 * BLK :] += lax.dot_general(high, high, nt, preferred_element_type=jnp.float32)

    for s in range(NSB):
        for t in range(NSB):
            if t == 2 and s < 2:
                block = total[2 * BLK :, s * BLK : (s + 1) * BLK].T
            else:
                block = total[s * BLK : (s + 1) * BLK, t * BLK : (t + 1) * BLK]
            ext[s * NSB + t] = block

    def put(ids, w, blocks):
        return sum(block * (ids[0, t] == w).astype(jnp.float32) for t, block in enumerate(blocks))

    def row(w):
        return [put(screen, w, [ext[s * NSB + t] for s in range(NSB)]) for t in range(NSB)]

    def rows(side, w):
        for t, block in enumerate(row(w)):
            side[w % BB_DEV, t] = block

    downs, ups = [], []
    for r in range(BB_DEV):
        downs.append(remote(out_prev.at[r], in_next.at[r], row_send.at[r], row_recv.at[r], me - 1))
        ups.append(remote(out_next.at[r], in_prev.at[r], row_send.at[2 + r], row_recv.at[2 + r], me + 1))
    for r in range(BB_DEV):
        rows(out_prev, r)

        @pl.when(has_prev)
        def _():
            downs[r].start()

        rows(out_next, 2 * BB_DEV + r)

        @pl.when(has_next)
        def _():
            ups[r].start()

    def place(r, j):
        return slice(r * BLK, (r + 1) * BLK), slice(j * BLK, (j + 1) * BLK)

    for r in range(BB_DEV):
        own_row = row(BB_DEV + r)
        for j in range(5 * BB_DEV):
            if BB_DEV <= j < 4 * BB_DEV:
                band[place(r, j)] = put(screen, j - BB_DEV, own_row)
            else:
                band[place(r, j)] = zero

    @pl.when(has_prev)
    def _():
        occ_down.wait_send()
        id_down.wait_send()
        id_up.wait_recv()
        for r in range(BB_DEV):
            ups[r].wait_recv()
        for r in range(BB_DEV):
            for j in range(3 * BB_DEV):
                band[place(r, j)] += put(ids_prev, j, [in_prev[r, t] for t in range(NSB)])

    @pl.when(has_next)
    def _():
        occ_up.wait_send()
        id_up.wait_send()
        id_down.wait_recv()
        for r in range(BB_DEV):
            downs[r].wait_recv()
        for r in range(BB_DEV):
            for j in range(3 * BB_DEV):
                band[place(r, j + 2 * BB_DEV)] += put(ids_next, j, [in_next[r, t] for t in range(NSB)])

    @pl.when(has_prev)
    def _():
        for r in range(BB_DEV):
            downs[r].wait_send()

    @pl.when(has_next)
    def _():
        for r in range(BB_DEV):
            ups[r].wait_send()


def solution(mesh):
    count = mesh.shape["aux"]

    def shards(integrals, coeff, screen, occ_ids):
        aux_rows = integrals.shape[0]
        ints = jnp.transpose(integrals, (0, 1, 3, 2, 4))
        vmem = pl.BlockSpec(memory_space=pltpu.VMEM)
        smem = pl.BlockSpec(memory_space=pltpu.SMEM)
        nocc = OCCB * BLK
        dma = pltpu.SemaphoreType.DMA
        return pl.pallas_call(
            lambda *refs: kernel(count, *refs),
            out_shape=jax.ShapeDtypeStruct((EDGE, 5 * EDGE), jnp.float32),
            in_specs=[pl.BlockSpec(memory_space=pl.ANY), vmem, smem, smem],
            out_specs=vmem,
            scratch_shapes=[
                pltpu.VMEM((aux_rows, NSB, NSB, BLK, BLK), jnp.bfloat16),
                pltpu.VMEM((3 * BB_DEV, BLK, nocc), jnp.bfloat16),
                pltpu.VMEM((NSB * BLK, nocc), jnp.bfloat16),
                pltpu.VMEM((NSB * BLK, NSB * BLK), jnp.float32),
                pltpu.VMEM((NSB * NSB, BLK, BLK), jnp.float32),
                pltpu.VMEM((BB_DEV, NSB, BLK, BLK), jnp.float32),
                pltpu.VMEM((BB_DEV, NSB, BLK, BLK), jnp.float32),
                pltpu.VMEM((BB_DEV, NSB, BLK, BLK), jnp.float32),
                pltpu.VMEM((BB_DEV, NSB, BLK, BLK), jnp.float32),
                pltpu.SMEM((1, NSB), jnp.int32),
                pltpu.SMEM((1, NSB), jnp.int32),
                dma((aux_rows // STEP,)),
                dma((2,)),
                dma((2,)),
                dma((2,)),
                dma((2,)),
                dma((4,)),
                dma((4,)),
            ],
            compiler_params=pltpu.CompilerParams(
                collective_id=0, has_side_effects=True, vmem_limit_bytes=40 * MIB),
            cost_estimate=pl.CostEstimate(
                flops=4 * aux_rows * NSB * BLK * NSB * BLK * nocc, transcendentals=0,
                bytes_accessed=aux_rows * (NSB * BLK) ** 2 * 2),
        )(ints, coeff, screen, occ_ids)

    return jax.shard_map(
        shards,
        mesh=mesh,
        in_specs=(
            P(("groups", "aux"), None, None, None, None),
            P(("groups", "aux"), None),
            P(("groups", "aux"), None),
            P("groups"),
        ),
        out_specs=P(("groups", "aux"), None),
        check_vma=False,
    )
```

time: 167 us -> 42.3 us (0.25)
  the two profiles are of different devices: /device:TPU:1 before, /device:TPU:20 now
where the time goes in v1:
time: 42.3 us; the launch traced here: 42.1 us
  Pallas kernels  35 us (83%)
  local copies, waits for them, and re-layouts  7.09 us (17%)
    pallas_call x1, Pallas kernels, shards(): pl.pallas_call(lambda *refs: kernel(count, *refs), out_shape=jax.ShapeDty...  35 us
    unnamed x9, local copies, waits for them, and re-layouts  7.09 us

profile of v1, /device:TPU:20, one launch (start us, length us, event | category | flops | bytes accessed | tf_op | source)
XLA Modules:
  0.0 42.1 jit_solution(16123265381221151427)
XLA Ops:
  0.0 0.0 copy-start
  0.0 3.7 %copy-done = bf16[32,3,128,3,128]{4,2,3,1,0:T(8,128)(2,1)S(1)} copy-done((bf16[32,3,128,3,128]{4,2,3,1,0:T(8,128)(2,1)S(1)}, bf16[32,3,128,3,128]{4,2,3,1,0:T(8,128)(2,1)}, u32[]{:S(2)}) %copy-start) | copy-done | bytes 9437208
  3.7 0.0 copy-start.1
  3.7 1.0 %copy-done.1 = bf16[256,1024]{1,0:T(8,128)(2,1)S(1)} copy-done((bf16[256,1024]{1,0:T(8,128)(2,1)S(1)}, bf16[256,1024]{1,0:T(8,128)(2,1)}, u32[]{:S(2)}) %copy-start.1) | copy-done | bytes 524312
  4.7 0.0 copy-start.2
  4.7 0.7 %copy-done.2 = s32[1,3]{1,0:T(1,128)S(1)} copy-done((s32[1,3]{1,0:T(1,128)S(1)}, s32[1,3]{1,0:T(1,128)}, u32[]{:S(2)}) %copy-start.2) | copy-done | bytes 36
  5.4 0.0 copy-start.3
  5.4 0.7 %copy-done.3 = s32[4]{0:T(128)S(1)} copy-done((s32[4]{0:T(128)S(1)}, s32[4]{0:T(128)}, u32[]{:S(2)}) %copy-start.3) | copy-done | bytes 40
  6.0 35.0 %shard_map.46 = f32[256,1280]{1,0:T(8,128)S(1)} custom-call(bf16[32,3,3,128,128]{4,3,2,1,0:T(8,128)(2,1)S(1)} %bitcast.1, bf16[256,1024]{1,0:T(8,128)(2,1)S(1)} %copy-done.1, s32[1,3]{1,0:T(1,128)S(1)} %copy-done.2, s32[4]{0:T(128)S(1)} %copy-done.3), custom_call_target="tpu_custom_call" | custom-call | flops 9663676416 | bytes 9437184 | tf_op jit(solution)/shard_map/pallas_call | solution.py:200
  41.0 1.1 %copy.6 = f32[256,1280]{1,0:T(8,128)} copy(f32[256,1280]{1,0:T(8,128)S(1)} %shard_map.46) | data formatting | bytes 2621440
Async XLA Ops:
  0.0 3.7 %copy-start = (bf16[32,3,128,3,128]{4,2,3,1,0:T(8,128)(2,1)S(1)}, bf16[32,3,128,3,128]{4,2,3,1,0:T(8,128)(2,1)}, u32[]{:S(2)}) copy-start(bf16[32,3,128,3,128]{4,2,3,1,0:T(8,128)(2,1)} %param.4) | copy-start | bytes 28311556
  3.7 1.0 %copy-start.1 = (bf16[256,1024]{1,0:T(8,128)(2,1)S(1)}, bf16[256,1024]{1,0:T(8,128)(2,1)}, u32[]{:S(2)}) copy-start(bf16[256,1024]{1,0:T(8,128)(2,1)} %refs_1_.1) | copy-start | bytes 1572868
  4.7 0.7 %copy-start.2 = (s32[1,3]{1,0:T(1,128)S(1)}, s32[1,3]{1,0:T(1,128)}, u32[]{:S(2)}) copy-start(s32[1,3]{1,0:T(1,128)} %refs_2_.1) | copy-start | bytes 40
  5.4 0.7 %copy-start.3 = (s32[4]{0:T(128)S(1)}, s32[4]{0:T(128)}, u32[]{:S(2)}) copy-start(s32[4]{0:T(128)} %refs_3_.1) | copy-start | bytes 52

commit v2 on v1

v2 whole, which is shorter than its diff:
```python
import jax
import jax.numpy as jnp
from jax import lax
from jax.experimental import pallas as pl
from jax.experimental.pallas import tpu as pltpu
from jax.sharding import PartitionSpec as P

BLK = 128
BB_DEV = 2
NSB = 3
OCCB = 4
OCCA_B = 8
EDGE = BB_DEV * BLK
STEP = 8
CUTS = 2
PART = OCCB // CUTS
MIB = 1 << 20
TOP = 46340.0


def kernel(count, ints, coeff_hbm, screen_hbm, occ_hbm, band, coeff, screen, occ_ids, buf, window, picked, total, ext, out_prev, out_next,
           in_prev, in_next, ids_prev, ids_next, load_sem, occ_send, occ_recv, id_send, id_recv, row_send, row_recv, arg_sem,
           unit_out, unit_prev, unit_next, unit_send, unit_recv):
    me = lax.axis_index("aux")
    has_prev, has_next = me > 0, me < count - 1
    aux_rows = ints.shape[0]
    steps = aux_rows // STEP

    fetches = [
        pltpu.make_async_copy(src, dst, arg_sem.at[i])
        for i, (src, dst) in enumerate([(occ_hbm, occ_ids), (coeff_hbm, coeff), (screen_hbm, screen)])
    ]
    for fetch in fetches:
        fetch.start()

    barrier = pltpu.get_barrier_semaphore()

    @pl.when(has_prev)
    def _():
        pl.semaphore_signal(barrier, inc=1, device_id={"aux": me - 1}, device_id_type=pl.DeviceIdType.MESH)

    @pl.when(has_next)
    def _():
        pl.semaphore_signal(barrier, inc=1, device_id={"aux": me + 1}, device_id_type=pl.DeviceIdType.MESH)

    def load(step):
        part = pl.ds(step * STEP, STEP)
        return pltpu.make_async_copy(ints.at[part], buf.at[part], load_sem.at[step])

    @pl.loop(0, steps)
    def _(step):
        load(step).start()

    for fetch in fetches:
        fetch.wait()

    def pick(index, blocks):
        return sum(block * (index == k).astype(jnp.float32).astype(block.dtype) for k, block in enumerate(blocks))

    def remote(src, dst, send, recv, device):
        return pltpu.make_async_remote_copy(
            src_ref=src, dst_ref=dst, send_sem=send, recv_sem=recv,
            device_id={"aux": device}, device_id_type=pl.DeviceIdType.MESH)

    occ_down, occ_up = [], []
    for cut in range(CUTS):
        own = window.at[cut, BB_DEV : 2 * BB_DEV]
        occ_down.append(remote(own, window.at[cut, 2 * BB_DEV : 3 * BB_DEV], occ_send.at[cut], occ_recv.at[cut], me - 1))
        occ_up.append(remote(own, window.at[cut, 0:BB_DEV], occ_send.at[CUTS + cut], occ_recv.at[CUTS + cut], me + 1))
    id_down = remote(screen, ids_next, id_send.at[0], id_recv.at[0], me - 1)
    id_up = remote(screen, ids_prev, id_send.at[1], id_recv.at[1], me + 1)

    for cut in range(CUTS):
        for c in range(PART):
            chosen = pick(occ_ids[cut * PART + c], [coeff[:, k * BLK : (k + 1) * BLK] for k in range(OCCA_B)])
            for r in range(BB_DEV):
                window[cut, BB_DEV + r, :, c * BLK : (c + 1) * BLK] = chosen[r * BLK : (r + 1) * BLK]
        if cut == 0:
            pl.semaphore_wait(barrier, has_prev.astype(jnp.int32) + has_next.astype(jnp.int32))

        @pl.when(has_prev)
        def _():
            occ_down[cut].start()
            if cut == CUTS - 1:
                id_down.start()

        @pl.when(has_next)
        def _():
            occ_up[cut].start()
            if cut == CUTS - 1:
                id_up.start()

    total[...] = jnp.zeros_like(total)
    zero = jnp.zeros((BLK, BLK), jnp.float32)
    blank = jnp.zeros((BB_DEV, BLK, PART * BLK), window.dtype)
    nt = (((1,), (1,)), ((), ()))
    for cut in range(CUTS):

        @pl.when(has_next)
        def _():
            occ_down[cut].wait_recv()

        @pl.when(jnp.logical_not(has_next))
        def _():
            window[cut, 2 * BB_DEV : 3 * BB_DEV] = blank

        @pl.when(has_prev)
        def _():
            occ_up[cut].wait_recv()

        @pl.when(jnp.logical_not(has_prev))
        def _():
            window[cut, 0:BB_DEV] = blank

        for t in range(NSB):
            picked[cut, t * BLK : (t + 1) * BLK] = pick(screen[0, t], [window[cut, w] for w in range(3 * BB_DEV)])

        @pl.loop(0, steps)
        def _(step):
            if cut == 0:
                load(step).wait()
            halves = []
            for p in range(STEP):
                x = buf[step * STEP + p]
                left = jnp.concatenate([x[:, t].reshape(NSB * BLK, BLK) for t in range(NSB)], axis=1)
                halves.append(jnp.dot(left, picked[cut], preferred_element_type=jnp.float32).astype(jnp.bfloat16))
            half = jnp.concatenate(halves, axis=1)
            low = half[: 2 * BLK]
            high = half[2 * BLK :]
            total[:, : 2 * BLK] += lax.dot_general(half, low, nt, preferred_element_type=jnp.float32)
            total[2 * BLK :, 2 * BLK :] += lax.dot_general(high, high, nt, preferred_element_type=jnp.float32)

    for s in range(NSB):
        for t in range(NSB):
            if t == 2 and s < 2:
                block = total[2 * BLK :, s * BLK : (s + 1) * BLK].T
            else:
                block = total[s * BLK : (s + 1) * BLK, t * BLK : (t + 1) * BLK]
            ext[s * NSB + t] = block

    def put(ids, w, blocks):
        return sum(block * (ids[0, t] == w).astype(jnp.float32) for t, block in enumerate(blocks))

    def row(w):
        return [put(screen, w, [ext[s * NSB + t] for s in range(NSB)]) for t in range(NSB)]

    def rows(side, w):
        for t, block in enumerate(row(w)):
            side[w % BB_DEV, t] = code(block)

    largest = jnp.maximum(ext[0], jnp.maximum(ext[NSB + 1], ext[2 * NSB + 2]))
    largest = jnp.maximum(jnp.max(largest, axis=(0, 1), keepdims=True), 1e-30)
    unit_out[...] = jnp.broadcast_to(largest * (1.0 / TOP), unit_out.shape)
    grow = TOP / largest

    def code(block):
        x = block * grow
        x2 = x * x
        return ((x2 * x2) * (x2 * (x * jnp.abs(x)))).astype(jnp.bfloat16)

    def decode(block, unit):
        y = block.astype(jnp.float32)
        root = lax.rsqrt(lax.rsqrt(jnp.maximum(jnp.abs(y), 1e-37)))
        root = root * lax.rsqrt(root) * unit[0:1]
        return jnp.where(y < 0, -root, jnp.where(y > 0, root, 0.0))

    unit_down = remote(unit_out, unit_next, unit_send.at[0], unit_recv.at[0], me - 1)
    unit_up = remote(unit_out, unit_prev, unit_send.at[1], unit_recv.at[1], me + 1)

    @pl.when(has_prev)
    def _():
        unit_down.start()

    @pl.when(has_next)
    def _():
        unit_up.start()

    downs, ups = [], []
    for r in range(BB_DEV):
        downs.append(remote(out_prev.at[r], in_next.at[r], row_send.at[r], row_recv.at[r], me - 1))
        ups.append(remote(out_next.at[r], in_prev.at[r], row_send.at[2 + r], row_recv.at[2 + r], me + 1))
    for r in range(BB_DEV):
        rows(out_prev, r)

        @pl.when(has_prev)
        def _():
            downs[r].start()

        rows(out_next, 2 * BB_DEV + r)

        @pl.when(has_next)
        def _():
            ups[r].start()

    def place(r, j):
        return slice(r * BLK, (r + 1) * BLK), slice(j * BLK, (j + 1) * BLK)

    for r in range(BB_DEV):
        own_row = row(BB_DEV + r)
        for j in range(5 * BB_DEV):
            if BB_DEV <= j < 4 * BB_DEV:
                band[place(r, j)] = put(screen, j - BB_DEV, own_row)
            else:
                band[place(r, j)] = zero

    @pl.when(has_prev)
    def _():
        for cut in range(CUTS):
            occ_down[cut].wait_send()
        id_down.wait_send()
        id_up.wait_recv()
        unit_down.wait_send()
        unit_up.wait_recv()
        for r in range(BB_DEV):
            ups[r].wait_recv()
        for r in range(BB_DEV):
            came = [decode(in_prev[r, t], unit_prev) for t in range(NSB)]
            for j in range(3 * BB_DEV):
                band[place(r, j)] += put(ids_prev, j, came)

    @pl.when(has_next)
    def _():
        for cut in range(CUTS):
            occ_up[cut].wait_send()
        id_up.wait_send()
        id_down.wait_recv()
        unit_up.wait_send()
        unit_down.wait_recv()
        for r in range(BB_DEV):
            downs[r].wait_recv()
        for r in range(BB_DEV):
            came = [decode(in_next[r, t], unit_next) for t in range(NSB)]
            for j in range(3 * BB_DEV):
                band[place(r, j + 2 * BB_DEV)] += put(ids_next, j, came)

    @pl.when(has_prev)
    def _():
        for r in range(BB_DEV):
            downs[r].wait_send()

    @pl.when(has_next)
    def _():
        for r in range(BB_DEV):
            ups[r].wait_send()


def solution(mesh):
    count = mesh.shape["aux"]

    def shards(integrals, coeff, screen, occ_ids):
        aux_rows = integrals.shape[0]
        ints = jnp.transpose(integrals, (0, 1, 3, 2, 4))
        vmem = pl.BlockSpec(memory_space=pltpu.VMEM)
        nocc = OCCB * BLK
        dma = pltpu.SemaphoreType.DMA
        return pl.pallas_call(
            lambda *refs: kernel(count, *refs),
            out_shape=jax.ShapeDtypeStruct((EDGE, 5 * EDGE), jnp.float32),
            in_specs=[pl.BlockSpec(memory_space=pltpu.HBM)] * 4,
            out_specs=vmem,
            scratch_shapes=[
                pltpu.VMEM(coeff.shape, coeff.dtype),
                pltpu.SMEM(screen.shape, screen.dtype),
                pltpu.SMEM(occ_ids.shape, occ_ids.dtype),
                pltpu.VMEM((aux_rows, NSB, NSB, BLK, BLK), jnp.bfloat16),
                pltpu.VMEM((CUTS, 3 * BB_DEV, BLK, PART * BLK), jnp.bfloat16),
                pltpu.VMEM((CUTS, NSB * BLK, PART * BLK), jnp.bfloat16),
                pltpu.VMEM((NSB * BLK, NSB * BLK), jnp.float32),
                pltpu.VMEM((NSB * NSB, BLK, BLK), jnp.float32),
                pltpu.VMEM((BB_DEV, NSB, BLK, BLK), jnp.bfloat16),
                pltpu.VMEM((BB_DEV, NSB, BLK, BLK), jnp.bfloat16),
                pltpu.VMEM((BB_DEV, NSB, BLK, BLK), jnp.bfloat16),
                pltpu.VMEM((BB_DEV, NSB, BLK, BLK), jnp.bfloat16),
                pltpu.SMEM((1, NSB), jnp.int32),
                pltpu.SMEM((1, NSB), jnp.int32),
                dma((aux_rows // STEP,)),
                dma((2 * CUTS,)),
                dma((2 * CUTS,)),
                dma((2,)),
                dma((2,)),
                dma((4,)),
                dma((4,)),
                dma((3,)),
                pltpu.VMEM((8, BLK), jnp.float32),
                pltpu.VMEM((8, BLK), jnp.float32),
                pltpu.VMEM((8, BLK), jnp.float32),
                dma((2,)),
                dma((2,)),
            ],
            compiler_params=pltpu.CompilerParams(
                collective_id=0, has_side_effects=True, vmem_limit_bytes=56 * MIB),
            cost_estimate=pl.CostEstimate(
                flops=4 * aux_rows * NSB * BLK * NSB * BLK * nocc, transcendentals=0,
                bytes_accessed=aux_rows * (NSB * BLK) ** 2 * 2),
        )(ints, coeff, screen, occ_ids)

    return jax.shard_map(
        shards,
        mesh=mesh,
        in_specs=(
            P(("groups", "aux"), None, None, None, None),
            P(("groups", "aux"), None),
            P(("groups", "aux"), None),
            P("groups"),
        ),
        out_specs=P(("groups", "aux"), None),
        check_vma=False,
    )
```

time: 42.3 us -> 30.1 us (0.71)
  the two profiles are of different devices: /device:TPU:20 before, /device:TPU:1 now
where the time goes in v2:
time: 30.1 us; the launch traced here: 29.9 us
  Pallas kernels  27.4 us (91%)
  local copies, waits for them, and re-layouts  2.46 us (8%)
    pallas_call x1, Pallas kernels, shards(): pl.pallas_call(lambda *refs: kernel(count, *refs), out_shape=jax.ShapeDty...  27.4 us
    unnamed x1, local copies, waits for them, and re-layouts  2.46 us

profile of v2, /device:TPU:1, one launch (start us, length us, event | category | flops | bytes accessed | tf_op | source)
XLA Modules:
  0.0 29.9 jit_solution(5020981092083308664)
XLA Ops:
  0.0 27.4 %shard_map.46 = f32[256,1280]{1,0:T(8,128)} custom-call(bf16[32,3,3,128,128]{4,3,2,1,0:T(8,128)(2,1)} %bitcast.1, bf16[256,1024]{1,0:T(8,128)(2,1)} %refs_1_.1, s32[1,3]{1,0:T(1,128)} %refs_2_.1, s32[4]{0:T(128)} %refs_3_.1), custom_call_target="tpu_custom_call" | custom-call | flops 9663676416 | bytes 9437184 | tf_op jit(solution)/shard_map/pallas_call | solution.py:256
  27.5 2.5 %copy.6 = f32[256,1280]{1,0:T(8,128)} copy(f32[256,1280]{1,0:T(8,128)} %shard_map.46) | data formatting | bytes 2621440

commit v3 on v2

--- a/solution.py
+++ b/solution.py
@@ -211,12 +211,6 @@
         id_up.wait_recv()
         unit_down.wait_send()
         unit_up.wait_recv()
-        for r in range(BB_DEV):
-            ups[r].wait_recv()
-        for r in range(BB_DEV):
-            came = [decode(in_prev[r, t], unit_prev) for t in range(NSB)]
-            for j in range(3 * BB_DEV):
-                band[place(r, j)] += put(ids_prev, j, came)
 
     @pl.when(has_next)
     def _():
@@ -226,9 +220,19 @@
         id_down.wait_recv()
         unit_up.wait_send()
         unit_down.wait_recv()
-        for r in range(BB_DEV):
+
+    for r in range(BB_DEV):
+
+        @pl.when(has_prev)
+        def _():
+            ups[r].wait_recv()
+            came = [decode(in_prev[r, t], unit_prev) for t in range(NSB)]
+            for j in range(3 * BB_DEV):
+                band[place(r, j)] += put(ids_prev, j, came)
+
+        @pl.when(has_next)
+        def _():
             downs[r].wait_recv()
-        for r in range(BB_DEV):
             came = [decode(in_next[r, t], unit_next) for t in range(NSB)]
             for j in range(3 * BB_DEV):
                 band[place(r, j + 2 * BB_DEV)] += put(ids_next, j, came)

time: 30.1 us -> 29.9 us (level)
  no operation moved by 1% of the time
where the time goes in v3:
time: 29.9 us; the launch traced here: 29.7 us
  Pallas kernels  27.3 us (91%)
  local copies, waits for them, and re-layouts  2.46 us (8%)
    pallas_call x1, Pallas kernels, shards(): pl.pallas_call(lambda *refs: kernel(count, *refs), out_shape=jax.ShapeDty...  27.3 us
    unnamed x1, local copies, waits for them, and re-layouts  2.46 us

profile of v3, /device:TPU:1, one launch (start us, length us, event | category | flops | bytes accessed | tf_op | source)
XLA Modules:
  0.0 29.7 jit_solution(6485926396053562385)
XLA Ops:
  0.0 27.3 %shard_map.46 = f32[256,1280]{1,0:T(8,128)} custom-call(bf16[32,3,3,128,128]{4,3,2,1,0:T(8,128)(2,1)} %bitcast.1, bf16[256,1024]{1,0:T(8,128)(2,1)} %refs_1_.1, s32[1,3]{1,0:T(1,128)} %refs_2_.1, s32[4]{0:T(128)} %refs_3_.1), custom_call_target="tpu_custom_call" | custom-call | flops 9663676416 | bytes 9437184 | tf_op jit(solution)/shard_map/pallas_call | solution.py:260
  27.3 2.5 %copy.6 = f32[256,1280]{1,0:T(8,128)} copy(f32[256,1280]{1,0:T(8,128)} %shard_map.46) | data formatting | bytes 2621440
